TPU v7x, 32 devices: a whole 2x2x4 slice. The times are simulated.
32 devices in a mesh: ctx: 16 (over z, x, core), tp: 2 (over y).
Axes of the slice: x: 2, y: 2, z: 4, core: 2. Of those that a mesh axis runs over, the one named last changes fastest.
Arguments:
- hyena_q: bfloat16 [2048, 8192], P('ctx', 'tp'), may hold values from -36 to 36
- hyena_k: bfloat16 [2048, 8192], P('ctx', 'tp'), may hold values from -6 to 6
- hyena_v: bfloat16 [2048, 8192], P('ctx', 'tp'), may hold values from -6 to 6
- filter_rate: float32 [8192, 16], P('tp'), may hold values from 0 to 1, as said below
- filter_residue: float32 [8192, 16], P('tp'), may hold values from -0.12 to 0.12
- skip_gain: float32 [8192], P('tp'), may hold values from 0.5 to 1.5
Outputs:
- hyena_out: bfloat16 [2048, 8192], P('ctx', 'tp')
Inputs may be any that keep to these rules, and one draw needn't show every extreme that they name: `filter_rate`: every rate is positive and at most 0.05.
All inputs are finite; a program needn't handle non-finite values.
Results may differ from a plain program's by a relative error of at most 0.0057.
Values may be sent and summed in bfloat16 or wider, within the bound.
A program may use at most 64 MiB of HBM per device.

v0:
```python
import functools

import jax
import jax.numpy as jnp
from jax import lax
from jax.experimental import pallas as pl
from jax.experimental.pallas import tpu as pltpu
from jax.sharding import PartitionSpec as P

D = 8192
ORDER = 16
LANES = 128
SUB = 8
WIDE = SUB * LANES
STEP = 16
MESH = pl.DeviceIdType.MESH


def kernel(
    n,
    ntp,
    n_own,
    q_hbm,
    k_hbm,
    v_hbm,
    rate_hbm,
    res_hbm,
    skip_hbm,
    gated_hbm,
    sums_ref,
    qv,
    kv,
    vv,
    gv,
    rate_v,
    res_v,
    skip_v,
    rate_s,
    res_s,
    decay_s,
    block_s,
    pos,
    fir,
    held,
    ends,
    ends_pair,
    chip_ends,
    ends_in,
    carry_out,
    carry_in,
    carry_pair,
    carry,
    squares,
    sums_own,
    sums_in,
    q_sem,
    k_sem,
    v_sem,
    g_sem,
    param_sem,
    pair_send,
    pair_recv,
    end_send,
    end_recv,
    carry_send,
    carry_recv,
    back_send,
    back_recv,
    sum_send,
    sum_recv,
):
    rows, width = q_hbm.shape
    groups = width // WIDE
    blocks = rows // STEP
    tiles = width // LANES
    chips = n // 2
    half = ORDER * groups // 2
    unit = min(ORDER, half)
    units = half // unit
    keep = unit // n_own
    spread = chips // n_own
    me = lax.axis_index("ctx")
    me_tp = lax.axis_index("tp")
    chip, core = me // 2, lax.rem(me, 2)
    pair = me + 1 - 2 * core
    own = chip // spread
    first = core * half
    first_pair = half - first
    early = core == 0

    def cols(g):
        return pl.ds(pl.multiple_of(g * WIDE, WIDE), WIDE)

    def load_copy(src, dst, sem, g):
        return pltpu.make_async_copy(src.at[:, cols(g)], dst.at[g], sem.at[g])

    def out_copy(g):
        return pltpu.make_async_copy(gv.at[g], gated_hbm.at[:, cols(g)], g_sem.at[g])

    def param_copy(which):
        src, dst = ((rate_hbm, rate_v), (res_hbm, res_v), (skip_hbm, skip_v))[which]
        return pltpu.make_async_copy(src, dst, param_sem.at[which])

    def first_group(j):
        whose = lax.rem(core + 1 + j, 2)
        return lax.rem(whose * (groups // 2) + j // 2, groups)

    def last_group(j):
        return lax.rem(core * (groups // 2) + j, groups)

    def remote(src, dst, send, recv, **where):
        return pltpu.make_async_remote_copy(
            src_ref=src,
            dst_ref=dst,
            send_sem=send,
            recv_sem=recv,
            device_id=where,
            device_id_type=MESH,
        )

    def pair_copy(u):
        return remote(
            ends.at[pl.ds(first_pair + u * unit, unit)],
            ends_pair.at[pl.ds(u * unit, unit)],
            pair_send.at[u],
            pair_recv.at[u],
            ctx=pair,
        )

    def end_copy(u, owner):
        return remote(
            chip_ends.at[pl.ds(u * unit + owner * keep, keep)],
            ends_in.at[u * chips + chip],
            end_send.at[u * n_own + owner],
            end_recv.at[u * chips + chip],
            ctx=owner * spread * 2 + core,
        )

    def end_arrival(u, sender):
        return remote(
            chip_ends.at[pl.ds(0, keep)],
            ends_in.at[u * chips + sender],
            end_send.at[0],
            end_recv.at[u * chips + sender],
            ctx=sender * 2 + core,
        )

    def carry_copy(u, target):
        return remote(
            carry_out.at[u * chips + target],
            carry_in.at[pl.ds(u * unit + own * keep, keep)],
            carry_send.at[u * chips + target],
            carry_recv.at[u * n_own + own],
            ctx=target * 2 + core,
        )

    def carry_arrival(u, owner):
        return remote(
            carry_out.at[0],
            carry_in.at[pl.ds(u * unit + owner * keep, keep)],
            carry_send.at[0],
            carry_recv.at[u * n_own + owner],
            ctx=owner * spread * 2 + core,
        )

    def back_copy(u):
        return remote(
            carry_pair.at[pl.ds(u * unit, unit)],
            carry.at[pl.ds(first + u * unit, unit)],
            back_send.at[u],
            back_recv.at[u],
            ctx=pair,
        )

    def back_arrival(u):
        return remote(
            carry_pair.at[pl.ds(u * unit, unit)],
            carry.at[pl.ds(first_pair + u * unit, unit)],
            back_send.at[u],
            back_recv.at[u],
            ctx=pair,
        )

    def sum_copy(target):
        return remote(
            sums_own,
            sums_in.at[me_tp],
            sum_send.at[target],
            sum_recv.at[me_tp],
            tp=target,
        )

    def sum_arrival(sender):
        return remote(
            sums_own,
            sums_in.at[sender],
            sum_send.at[0],
            sum_recv.at[sender],
            tp=sender,
        )

    param_copy(0).start()

    def load_group(j, _):
        g = first_group(j)
        load_copy(k_hbm, kv, k_sem, g).start()
        load_copy(v_hbm, vv, v_sem, g).start()
        return 0

    lax.fori_loop(0, groups, load_group, 0)
    param_copy(1).start()
    param_copy(2).start()

    def load_gate(j, _):
        load_copy(q_hbm, qv, q_sem, last_group(j)).start()
        return 0

    lax.fori_loop(0, groups, load_gate, 0)

    barrier = pltpu.get_barrier_semaphore()

    def greet(**where):
        pl.semaphore_signal(barrier, inc=1, device_id=where, device_id_type=MESH)

    def greet_chip(d, _):
        @pl.when(d != chip)
        def _():
            greet(ctx=d * 2 + core)

        return 0

    def greet_tp(d, _):
        @pl.when(d != me_tp)
        def _():
            greet(tp=d)

        return 0

    greet(ctx=pair)
    lax.fori_loop(0, chips, greet_chip, 0)
    lax.fori_loop(0, ntp, greet_tp, 0)

    def spread_tiles(src, dst):
        for tile in range(tiles):
            lanes = slice(tile * LANES, (tile + 1) * LANES)
            dst[pl.ds(tile * (ORDER + 1), ORDER), :] = src[:, lanes]

    param_copy(0).wait()
    spread_tiles(rate_v, rate_s)

    def mode_row(ref, g, mode):
        pitch = ORDER + 1
        return ref[pl.ds(g * (SUB * pitch) + mode, SUB, stride=pitch), :]

    def row_power(row, power):
        return jnp.exp(-float(power) * mode_row(rate_s, row // ORDER, row % ORDER))

    def position(g, t):
        return pl.ds(g * (SUB * (rows + 1)) + t, SUB, stride=rows + 1)

    def tile_rows(g, tile):
        return pl.ds((g * SUB + tile) * (rows + 1), rows)

    def chip_unit(u):
        pair_copy(u).wait_recv()
        for r in range(unit):
            row = u * unit + r
            mine, theirs = ends[first + row], ends_pair[row]
            before = jnp.where(early, mine, theirs)
            after = jnp.where(early, theirs, mine)
            chip_ends[row] = before * row_power(first + row, rows) + after
        for owner in range(n_own):

            @pl.when(owner * spread != chip)
            def _():
                end_copy(u, owner).start()

    def local_states(j, _):
        g = first_group(j)
        load_copy(k_hbm, kv, k_sem, g).wait()
        load_copy(v_hbm, vv, v_sem, g).wait()
        for tile in range(SUB):
            lanes = slice(tile * LANES, (tile + 1) * LANES)
            wide = kv[g, :, lanes].astype(jnp.float32) * vv[g, :, lanes].astype(
                jnp.float32
            )
            pos[tile_rows(g, tile), :] = wide.astype(jnp.bfloat16).astype(jnp.float32)
        decay = []
        for mode in range(ORDER):
            rate = mode_row(rate_s, g, mode)
            decay.append(jnp.exp(-rate))
            decay_s[g, mode] = decay[mode]
            block_s[mode] = jnp.exp(-float(STEP) * rate)

        def block(b, totals):
            states = [pos[position(g, b * STEP), :]] * ORDER
            for i in range(1, STEP):
                here = pos[position(g, b * STEP + i), :]
                for mode in range(ORDER):
                    states[mode] = states[mode] * decay[mode] + here
            for mode in range(ORDER):
                held[g, b, mode] = states[mode]
            return tuple(
                totals[mode] * block_s[mode] + states[mode] for mode in range(ORDER)
            )

        zero = jnp.zeros((SUB, LANES), jnp.float32)
        totals = lax.fori_loop(0, blocks, block, (zero,) * ORDER)
        for mode in range(ORDER):
            ends[g * ORDER + mode] = totals[mode]

        @pl.when(j == 0)
        def _():
            pl.semaphore_wait(barrier, chips + ntp - 1)

        if groups > 1:

            @pl.when(lax.rem(j, 2) == 0)
            def _():
                pair_copy(j // 2).start()

            @pl.when(lax.rem(j, 2) == 1)
            def _():
                chip_unit(j // 2)

        return 0

    lax.fori_loop(0, groups, local_states, 0)
    if groups == 1:
        pair_copy(0).start()
        chip_unit(0)

    param_copy(1).wait()
    param_copy(2).wait()
    spread_tiles(res_v, res_s)

    def near(g, _):
        skip = skip_v[pl.ds(pl.multiple_of(g * SUB, SUB), SUB), :]
        weights = [mode_row(res_s, g, mode) for mode in range(ORDER)]
        taps = []
        for i in range(STEP):
            tap = functools.reduce(lambda x, y: x + y, weights)
            taps.append(tap + skip if i == 0 else tap)
            if i < STEP - 1:
                weights = [weights[mode] * decay_s[g, mode] for mode in range(ORDER)]

        def block(b, _):
            here = [pos[position(g, b * STEP + i), :] for i in range(STEP)]
            for i in range(STEP):
                total = taps[0] * here[i]
                for back in range(1, i + 1):
                    total = total + taps[back] * here[i - back]
                fir[g, b * STEP + i] = total
            for mode in range(ORDER):
                held[g, b, mode] = held[g, b, mode] * mode_row(res_s, g, mode)
            return 0

        lax.fori_loop(0, blocks, block, 0)
        return 0

    def own_scan(u):
        mine = u * unit + own * keep
        far = [row_power(first + mine + r, 2 * rows) for r in range(keep)]
        ends_in[u * chips + chip] = chip_ends[pl.ds(mine, keep)]

        def one(d, states):
            states = list(states)
            for r in range(keep):
                carry_out[u * chips + d, r] = states[r]

            @pl.when(d != chip)
            def _():
                carry_copy(u, d).start()
                end_arrival(u, d).wait_recv()

            for r in range(keep):
                states[r] = states[r] * far[r] + ends_in[u * chips + d, r]
            return tuple(states)

        zero = jnp.zeros((SUB, LANES), jnp.float32)
        lax.fori_loop(0, chips, one, (zero,) * keep)
        carry_in[pl.ds(mine, keep)] = carry_out[u * chips + chip]

    def scan(u):
        if spread == 1:
            own_scan(u)
        else:
            pl.when(lax.rem(chip, spread) == 0)(lambda: own_scan(u))

    lax.fori_loop(0, 1, near, 0)
    scan(0)
    for u in range(1, units):
        lax.fori_loop(2 * u - 1, 2 * u + 1, near, 0)
        scan(u)
    if groups > 1:
        lax.fori_loop(2 * units - 1, groups, near, 0)

    def take_unit(u):
        for owner in range(n_own):

            @pl.when(owner * spread != chip)
            def _():
                carry_arrival(u, owner).wait_recv()

        for r in range(unit):
            row = u * unit + r
            state = carry_in[row]
            before = jnp.where(early, ends[first + row], ends_pair[row])
            later = state * row_power(first + row, rows) + before
            carry[first + row] = jnp.where(early, state, later)
            carry_pair[row] = jnp.where(early, later, state)
        back_copy(u).start()

    squares[...] = jnp.zeros_like(squares)

    def finish(j, _):
        g = last_group(j)
        if groups > 1:
            pl.when(j < units)(lambda: take_unit(j))

            @pl.when(j >= units)
            def _():
                back_arrival(j - units).wait_recv()

        else:
            take_unit(0)
            back_arrival(0).wait_recv()
        decay = [decay_s[g, mode] for mode in range(ORDER)]

        def block(b, terms):
            terms = list(terms)
            for i in range(STEP):
                terms = [terms[mode] * decay[mode] for mode in range(ORDER)]
                tree = [fir[g, b * STEP + i]] + terms
                while len(tree) > 1:
                    pairs = [
                        tree[x] + tree[x + 1] for x in range(0, len(tree) - 1, 2)
                    ]
                    tree = pairs + tree[len(tree) // 2 * 2 :]
                pos[position(g, b * STEP + i), :] = tree[0]
            return tuple(terms[mode] + held[g, b, mode] for mode in range(ORDER))

        start = tuple(
            mode_row(res_s, g, mode) * carry[g * ORDER + mode] for mode in range(ORDER)
        )
        lax.fori_loop(0, blocks, block, start)
        load_copy(q_hbm, qv, q_sem, g).wait()
        for tile in range(SUB):
            lanes = slice(tile * LANES, (tile + 1) * LANES)
            gated = (
                qv[g, :, lanes].astype(jnp.float32) * pos[tile_rows(g, tile), :]
            ).astype(jnp.bfloat16)
            gv[g, :, lanes] = gated
            wide = gated.astype(jnp.float32)
            squares[...] += wide * wide
        out_copy(g).start()
        return 0

    lax.fori_loop(0, groups, finish, 0)

    sums_own[...] = lax.dot_general(
        jnp.ones((SUB, LANES), jnp.float32),
        squares[...],
        (((1,), (1,)), ((), ())),
        precision=lax.Precision.HIGHEST,
        preferred_element_type=jnp.float32,
    )

    def send_sum(d, _):
        @pl.when(d != me_tp)
        def _():
            sum_copy(d).start()

        return 0

    lax.fori_loop(0, ntp, send_sum, 0)
    sums_in[me_tp] = sums_own[...]

    def drain_out(g, _):
        out_copy(g).wait()
        return 0

    lax.fori_loop(0, groups, drain_out, 0)

    def drain_units(u, _):
        pair_copy(u).wait_send()
        back_copy(u).wait_send()
        return 0

    lax.fori_loop(0, units, drain_units, 0)

    def drain_ends(i, _):
        u, owner = i // n_own, lax.rem(i, n_own)

        @pl.when(owner * spread != chip)
        def _():
            end_copy(u, owner).wait_send()

        return 0

    lax.fori_loop(0, units * n_own, drain_ends, 0)

    def drain_carry():
        def one(i, _):
            u, d = i // chips, lax.rem(i, chips)

            @pl.when(d != chip)
            def _():
                carry_copy(u, d).wait_send()

            return 0

        lax.fori_loop(0, units * chips, one, 0)

    if spread == 1:
        drain_carry()
    else:
        pl.when(lax.rem(chip, spread) == 0)(drain_carry)

    def take_sum(d, _):
        @pl.when(d != me_tp)
        def _():
            sum_arrival(d).wait_recv()
            sum_copy(d).wait_send()

        return 0

    lax.fori_loop(0, ntp, take_sum, 0)
    total = sums_in[0]
    for d in range(1, ntp):
        total = total + sums_in[d]
    sums_ref[...] = total


def normalize(gated_hbm, sums_hbm, out_hbm, gv, ov, sums, scale, g_sem, o_sem, s_sem):
    groups = gv.shape[0]

    def part(j):
        return slice(j * WIDE, (j + 1) * WIDE)

    take = pltpu.make_async_copy(sums_hbm, sums, s_sem)
    take.start()
    reads = [
        pltpu.make_async_copy(gated_hbm.at[:, part(j)], gv.at[j], g_sem.at[j])
        for j in range(groups)
    ]
    writes = [
        pltpu.make_async_copy(ov.at[j], out_hbm.at[:, part(j)], o_sem.at[j])
        for j in range(groups)
    ]
    for read in reads:
        read.start()
    take.wait()
    root = jnp.sqrt(sums[0:1, :] / D + 1e-06)
    scale[...] = jnp.broadcast_to(1.0 / root, (LANES, scale.shape[0])).T
    for j in range(groups):
        reads[j].wait()
        for tile in range(SUB):
            lanes = slice(tile * LANES, (tile + 1) * LANES)
            wide = gv[j, :, lanes].astype(jnp.float32) * scale[...]
            ov[j, :, lanes] = wide.astype(jnp.bfloat16)
        writes[j].start()
    for write in writes:
        write.wait()


def per_device(n, ntp, hyena_q, hyena_k, hyena_v, filter_rate, filter_residue, skip):
    rows, width = hyena_q.shape
    groups = width // WIDE
    chips = n // 2
    half = ORDER * groups // 2
    unit = min(ORDER, half)
    units = half // unit
    n_own = min(chips, unit)
    keep = unit // n_own
    tiles = width // LANES
    f32, bf16 = jnp.float32, jnp.bfloat16
    any_space = pl.BlockSpec(memory_space=pl.ANY)
    hbm = pl.BlockSpec(memory_space=pltpu.HBM)
    vmem = pl.BlockSpec(memory_space=pltpu.VMEM)
    dma = pltpu.SemaphoreType.DMA
    gated, sums = pl.pallas_call(
        functools.partial(kernel, n, ntp, n_own),
        out_shape=(
            jax.ShapeDtypeStruct((rows, width), bf16),
            jax.ShapeDtypeStruct((SUB, rows), f32),
        ),
        in_specs=[hbm] * 6,
        out_specs=(any_space, vmem),
        scratch_shapes=[
            pltpu.VMEM((groups, rows, WIDE), bf16),
            pltpu.VMEM((groups, rows, WIDE), bf16),
            pltpu.VMEM((groups, rows, WIDE), bf16),
            pltpu.VMEM((groups, rows, WIDE), bf16),
            pltpu.VMEM((ORDER, width), f32),
            pltpu.VMEM((ORDER, width), f32),
            pltpu.VMEM((tiles, LANES), f32),
            pltpu.VMEM(((tiles + 1) * (ORDER + 1), LANES), f32),
            pltpu.VMEM(((tiles + 1) * (ORDER + 1), LANES), f32),
            pltpu.VMEM((groups, ORDER, SUB, LANES), f32),
            pltpu.VMEM((ORDER, SUB, LANES), f32),
            pltpu.VMEM(((tiles + 1) * (rows + 1), LANES), f32),
            pltpu.VMEM((groups, rows, SUB, LANES), f32),
            pltpu.VMEM((groups, rows // STEP, ORDER, SUB, LANES), f32),
            pltpu.VMEM((2 * half, SUB, LANES), f32),
            pltpu.VMEM((half, SUB, LANES), f32),
            pltpu.VMEM((half, SUB, LANES), f32),
            pltpu.VMEM((units * chips, keep, SUB, LANES), f32),
            pltpu.VMEM((units * chips, keep, SUB, LANES), f32),
            pltpu.VMEM((half, SUB, LANES), f32),
            pltpu.VMEM((half, SUB, LANES), f32),
            pltpu.VMEM((2 * half, SUB, LANES), f32),
            pltpu.VMEM((rows, LANES), f32),
            pltpu.VMEM((SUB, rows), f32),
            pltpu.VMEM((ntp, SUB, rows), f32),
            dma((groups,)),
            dma((groups,)),
            dma((groups,)),
            dma((groups,)),
            dma((3,)),
            dma((units,)),
            dma((units,)),
            dma((units * n_own,)),
            dma((units * chips,)),
            dma((units * chips,)),
            dma((units * n_own,)),
            dma((units,)),
            dma((units,)),
            dma((ntp,)),
            dma((ntp,)),
        ],
        compiler_params=pltpu.CompilerParams(
            collective_id=0,
            has_side_effects=True,
            vmem_limit_bytes=64 * 1024 * 1024 - 131072,
        ),
        cost_estimate=pl.CostEstimate(
            flops=5 * ORDER * rows * width,
            bytes_accessed=8 * rows * width,
            transcendentals=ORDER * width,
        ),
    )(
        hyena_q,
        hyena_k,
        hyena_v,
        filter_rate.T,
        filter_residue.T,
        skip.reshape(tiles, LANES),
    )
    return pl.pallas_call(
        normalize,
        out_shape=jax.ShapeDtypeStruct((rows, width), bf16),
        in_specs=[any_space, any_space],
        out_specs=any_space,
        scratch_shapes=[
            pltpu.VMEM((groups, rows, WIDE), bf16),
            pltpu.VMEM((groups, rows, WIDE), bf16),
            pltpu.VMEM((SUB, rows), f32),
            pltpu.VMEM((rows, LANES), f32),
            dma((groups,)),
            dma((groups,)),
            dma(()),
        ],
        compiler_params=pltpu.CompilerParams(
            vmem_limit_bytes=64 * 1024 * 1024 - 131072
        ),
    )(gated, sums)


def solution(mesh):
    n, ntp = mesh.shape["ctx"], mesh.shape["tp"]
    in_specs = (
        P("ctx", "tp"),
        P("ctx", "tp"),
        P("ctx", "tp"),
        P("tp", None),
        P("tp", None),
        P("tp"),
    )
    return jax.shard_map(
        functools.partial(per_device, n, ntp),
        mesh=mesh,
        in_specs=in_specs,
        out_specs=P("ctx", "tp"),
        check_vma=False,
    )
```

profile of v0, /device:TPU:0, one launch (start us, length us, event | category | flops | bytes accessed | tf_op | source)
XLA Modules:
  0.0 25.9 jit_solution(343291983397078992)
XLA Ops:
  0.0 23.8 %shard_map.64 = (bf16[128,4096]{1,0:T(8,128)(2,1)}, f32[8,128]{1,0:T(8,128)}) custom-call(bf16[128,4096]{1,0:T(8,128)(2,1)} %q_hbm.1, bf16[128,4096]{1,0:T(8,128)(2,1)} %k_hbm.1, bf16[128,4096]{1,0:T(8,128)(2,1)} %v_hbm.1, f32[16,4096]{1,0:T(8,128)} %bitcast.3, f32[16,4096]{1,0:T(8,128)} %bitcast.4, f32[32,128]{1,0:T(8,128)} %bitcast.5), custom_call_target="tpu_custom_call" | custom-call | flops 41943040 | bytes 4194304 | tf_op jit(solution)/shard_map/pallas_call | solution.py:582
  23.8 2.1 %shard_map.65 = bf16[128,4096]{1,0:T(8,128)(2,1)} custom-call(bf16[128,4096]{1,0:T(8,128)(2,1)} %get-tuple-element.7.gated_hbm, f32[8,128]{1,0:T(8,128)} %get-tuple-element.8.sums_hbm), custom_call_target="tpu_custom_call" | custom-call | tf_op jit(solution)/shard_map/pallas_call | solution.py:650
where the time goes:
time: 26.1 us; the launch traced here: 25.9 us
  Pallas kernels  25.9 us (99%)
    pallas_call x1, Pallas kernels, per_device(): pl.pallas_call(functools.partial(kernel, n, ntp, n_own), out_shape=(jax.S...  23.8 us
    pallas_call x1, Pallas kernels, per_device(): pl.pallas_call(normalize, out_shape=jax.ShapeDtypeStruct((rows, width), b...  2.14 us

commit v1 on v0

--- a/solution.py
+++ b/solution.py
@@ -390,10 +390,10 @@
     lax.fori_loop(0, 1, near, 0)
     scan(0)
     for u in range(1, units):
-        lax.fori_loop(2 * u - 1, 2 * u + 1, near, 0)
+        lax.fori_loop(u, u + 1, near, 0)
         scan(u)
     if groups > 1:
-        lax.fori_loop(2 * units - 1, groups, near, 0)
+        lax.fori_loop(units, groups, near, 0)
 
     def take_unit(u):
         for owner in range(n_own):

time: 26.1 us -> 25.8 us (0.989)
  Pallas kernels: 25.9 us -> 25.6 us
    pallas_call x1, Pallas kernels: 23.8 us -> 23.5 us  [per_device(): pl.pallas_call(functools.partial(kernel, n, ntp, n_own), out_shape=(jax.S...]
where the time goes in v1:
time: 25.8 us; the launch traced here: 25.6 us
  Pallas kernels  25.6 us (99%)
    pallas_call x1, Pallas kernels, per_device(): pl.pallas_call(functools.partial(kernel, n, ntp, n_own), out_shape=(jax.S...  23.5 us
    pallas_call x1, Pallas kernels, per_device(): pl.pallas_call(normalize, out_shape=jax.ShapeDtypeStruct((rows, width), b...  2.14 us

profile of v1, /device:TPU:0, one launch (start us, length us, event | category | flops | bytes accessed | tf_op | source)
XLA Modules:
  0.0 25.6 jit_solution(11167803670671843999)
XLA Ops:
  0.0 23.5 %shard_map.64 = (bf16[128,4096]{1,0:T(8,128)(2,1)}, f32[8,128]{1,0:T(8,128)}) custom-call(bf16[128,4096]{1,0:T(8,128)(2,1)} %q_hbm.1, bf16[128,4096]{1,0:T(8,128)(2,1)} %k_hbm.1, bf16[128,4096]{1,0:T(8,128)(2,1)} %v_hbm.1, f32[16,4096]{1,0:T(8,128)} %bitcast.3, f32[16,4096]{1,0:T(8,128)} %bitcast.4, f32[32,128]{1,0:T(8,128)} %bitcast.5), custom_call_target="tpu_custom_call" | custom-call | flops 41943040 | bytes 4194304 | tf_op jit(solution)/shard_map/pallas_call | solution.py:582
  23.5 2.1 %shard_map.65 = bf16[128,4096]{1,0:T(8,128)(2,1)} custom-call(bf16[128,4096]{1,0:T(8,128)(2,1)} %get-tuple-element.7.gated_hbm, f32[8,128]{1,0:T(8,128)} %get-tuple-element.8.sums_hbm), custom_call_target="tpu_custom_call" | custom-call | tf_op jit(solution)/shard_map/pallas_call | solution.py:650

commit v2 on v1

--- a/solution.py
+++ b/solution.py
@@ -12,7 +12,7 @@
 LANES = 128
 SUB = 8
 WIDE = SUB * LANES
-STEP = 16
+STEP = 8
 MESH = pl.DeviceIdType.MESH
 
 

time: 25.8 us -> 25.6 us (level)
  no operation moved by 1% of the time
where the time goes in v2:
time: 25.6 us; the launch traced here: 25.5 us
  Pallas kernels  25.5 us (100%)
    pallas_call x1, Pallas kernels, per_device(): pl.pallas_call(functools.partial(kernel, n, ntp, n_own), out_shape=(jax.S...  23.3 us
    pallas_call x1, Pallas kernels, per_device(): pl.pallas_call(normalize, out_shape=jax.ShapeDtypeStruct((rows, width), b...  2.14 us

profile of v2, /device:TPU:0, one launch (start us, length us, event | category | flops | bytes accessed | tf_op | source)
XLA Modules:
  0.0 25.5 jit_solution(16106373552827264701)
XLA Ops:
  0.0 23.3 %shard_map.64 = (bf16[128,4096]{1,0:T(8,128)(2,1)}, f32[8,128]{1,0:T(8,128)}) custom-call(bf16[128,4096]{1,0:T(8,128)(2,1)} %q_hbm.1, bf16[128,4096]{1,0:T(8,128)(2,1)} %k_hbm.1, bf16[128,4096]{1,0:T(8,128)(2,1)} %v_hbm.1, f32[16,4096]{1,0:T(8,128)} %bitcast.3, f32[16,4096]{1,0:T(8,128)} %bitcast.4, f32[32,128]{1,0:T(8,128)} %bitcast.5), custom_call_target="tpu_custom_call" | custom-call | flops 41943040 | bytes 4194304 | tf_op jit(solution)/shard_map/pallas_call | solution.py:582
  23.3 2.1 %shard_map.65 = bf16[128,4096]{1,0:T(8,128)(2,1)} custom-call(bf16[128,4096]{1,0:T(8,128)(2,1)} %get-tuple-element.7.gated_hbm, f32[8,128]{1,0:T(8,128)} %get-tuple-element.8.sums_hbm), custom_call_target="tpu_custom_call" | custom-call | tf_op jit(solution)/shard_map/pallas_call | solution.py:650
